TPU v7x, 32 devices: a whole 2x2x4 slice. The times are simulated.
32 devices in a mesh: shot: 2 (over x), freq: 8 (over z, y), tile: 2 (over core).
Axes of the slice: x: 2, y: 2, z: 4, core: 2. Of those that a mesh axis runs over, the one named last changes fastest.
Arguments:
- source_field: float32 [4, 8, 64, 1024], P('shot', 'freq', 'tile'), parts along dimension 0, may hold values from -6 to 6
- receiver_field: float32 [4, 8, 64, 1024], P('shot', 'freq', 'tile'), parts along dimension 0, may hold values from -6 to 6
- slowness: float32 [3, 64, 1024], P(None, 'tile', 'freq'), may hold values from 0.5 to 2
- omegas: float32 [8], P('freq'), may hold values from 1.5 to 5
Outputs:
- image_steps: float32 [6, 64, 1024], P('shot', 'tile'), parts along dimension 0
- illumination: float32 [6, 64, 1024], P('shot', 'tile'), parts along dimension 0
There are 2 independent parts, one for each index of `shot`. A program takes and returns all parts, laid end to end along the dimension named above; an argument that names none is the same for every part. Nothing has to cross between parts.
All inputs are finite; a program needn't handle non-finite values.
Results may differ from a plain program's by a relative error of at most 0.0003.
Values sent between devices are 32-bit elements; how exact they have to be, the bound alone decides.
No kernel may reach another device: no remote copies, remote signals or barrier semaphores. Data moves between devices by JAX's collectives and lax.ppermute only.
A program may use at most 64 MiB of HBM per device.

v0:
```python
import math

import jax
import jax.numpy as jnp
from jax import lax
from jax.experimental import pallas as pl
from jax.experimental.pallas import tpu as pltpu
from jax.sharding import PartitionSpec as P

STEPS = 3
TERMS = 10
NODES = 16
MARGIN = TERMS - 1
LANES = 128
ROWS = 8

LARGEST = 10.02
DEGREE = 11


def node_sum(order, product):
    wave = math.cos if order % 2 == 0 else math.sin
    weight = (1.0 if order == 0 else 2.0) / NODES
    angles = [math.pi * (m + 0.5) / NODES for m in range(NODES)]
    return weight * math.fsum(wave(product * math.cos(t)) * math.cos(order * t) for t in angles)


def polynomial(order):
    count = 64
    angles = [math.pi * (k + 0.5) / count for k in range(count)]
    samples = []
    for angle in angles:
        product = LARGEST * math.sqrt(0.5 * (math.cos(angle) + 1.0))
        value = node_sum(order, product)
        samples.append(value if order % 2 == 0 else value / product)
    cheb = [
        (1.0 if n == 0 else 2.0) / count * math.fsum(s * math.cos(n * t) for s, t in zip(samples, angles))
        for n in range(DEGREE + 1)
    ]
    powers = [0.0] * (DEGREE + 1)
    before, here = [1.0], [0.0, 1.0]
    for n in range(DEGREE + 1):
        now = before if n == 0 else here
        for k, c in enumerate(now):
            powers[k] += cheb[n] * c
        if n >= 1:
            after = [0.0] + [2.0 * c for c in here]
            for k, c in enumerate(before):
                after[k] -= c
            before, here = here, after
    return powers


ROOTS = (0.0, 0.95, 0.4, 0.75)


def basis_change():
    half = TERMS // 2

    def times(poly, factor):
        out = [0.0] * (len(poly) + len(factor) - 1)
        for i, a in enumerate(poly):
            for j, b in enumerate(factor):
                out[i + j] += a * b
        return out

    basis = [[1.0]]
    for n in range(1, TERMS):
        if n % 2 == 1:
            basis.append(times(basis[-1], [0.0, 8.0]))
        else:
            basis.append(times(basis[n - 2], [-64.0 * ROOTS[n // 2 - 1], 0.0, 64.0]))
    cheb = [[1.0], [0.0, 1.0]]
    for n in range(2, TERMS):
        new = [0.0] + [2.0 * c for c in cheb[-1]]
        for k, c in enumerate(cheb[n - 2]):
            new[k] -= c
        cheb.append(new)
    change = [[0.0] * TERMS for _ in range(TERMS)]
    for n in range(TERMS):
        rest = list(cheb[n])
        for k in range(n, -1, -2):
            factor = rest[k] / basis[k][k]
            change[k][n] = factor
            for i, c in enumerate(basis[k]):
                rest[i] -= factor * c
    return change


CHANGE = basis_change()
CHEBYSHEV = [polynomial(n) for n in range(TERMS)]
POLYNOMIALS = [
    [math.fsum(CHANGE[k][n] * CHEBYSHEV[n][i] for n in range(k % 2, TERMS, 2)) for i in range(DEGREE + 1)]
    for k in range(TERMS)
]


def blocks_for(rows, most):
    return min(most, -(-rows // ROWS))


class Layout:
    def __init__(self, depth, tile_rows, width):
        self.depth = depth
        self.last = depth == STEPS - 1
        self.own = tile_rows // ROWS
        self.total = 2 * self.own
        self.width = width
        self.columns = width // LANES
        self.out_rows = tile_rows + MARGIN * (STEPS - 1 - depth)
        self.out_blocks = blocks_for(self.out_rows, self.total)

    def blocks(self, n):
        return blocks_for(self.out_rows + MARGIN - n, self.total)

    def state(self, n):
        return (4, self.blocks(n), ROWS, self.width)


def cols(j):
    return slice(j * LANES, (j + 1) * LANES)


def rows_at(block):
    return pl.ds(pl.multiple_of(block * ROWS, ROWS), ROWS)


class Order:
    def __init__(self, layout):
        self.layout = layout
        self.tile = lax.axis_index("tile")
        row = lax.broadcasted_iota(jnp.int32, (ROWS, LANES), 0)
        self.index = jnp.where(self.tile == 0, row, ROWS - 1 - row)

    def flip(self, x):
        return jnp.take_along_axis(x, self.index, axis=0)

    def own(self, b):
        return jnp.where(self.tile == 0, b, self.layout.own - 1 - b)

    def other(self, b):
        return jnp.where(self.tile == 0, b - self.layout.own, self.layout.total - 1 - b)


def recursion(layout, terms):
    lane = lax.broadcasted_iota(jnp.int32, (ROWS, LANES), 1)
    row = lax.broadcasted_iota(jnp.int32, (ROWS, LANES), 0)
    lane_first, lane_last = lane == 0, lane == LANES - 1
    row_first, row_last = row == 0, row == ROWS - 1
    zero = jnp.zeros((ROWS, LANES), jnp.float32)
    columns = range(layout.columns)

    def one_pass(n, c):
            source, count, have = terms[n - 1], layout.blocks(n), layout.blocks(n - 1)
            here = [source[c, 0, :, cols(j)] for j in columns]
            here_up = [pltpu.roll(x, ROWS - 1, 0) for x in here]
            before = here
            for b in range(count):
                if b + 1 < have:
                    below = [source[c, b + 1, :, cols(j)] for j in columns]
                    below_up = [pltpu.roll(x, ROWS - 1, 0) for x in below]
                else:
                    below = below_up = [zero] * layout.columns
                pairs = [p + jnp.where(row_last, q, r) for p, q, r in zip(here, below_up, here_up)]
                pairs_down = [pltpu.roll(u, 1, 0) for u in pairs]
                x = [u + jnp.where(row_first, q, r) for u, q, r in zip(pairs, before, pairs_down)]
                before = pairs_down
                x_left = [pltpu.roll(v, LANES - 1, 1) for v in x] + [zero]
                x_right = [pltpu.roll(v, 1, 1) for v in x] + [zero]
                wide = [
                    (x[j] + x[j])
                    + (
                        jnp.where(lane_last, x_left[j + 1], x_left[j])
                        + jnp.where(lane_first, x_right[j - 1], x_right[j])
                    )
                    for j in columns
                ]
                for j in columns:
                    value = wide[j] - 8.0 * here[j]
                    if n % 2 == 0 and ROOTS[n // 2 - 1] != 0.0:
                        value = value - (64.0 * ROOTS[n // 2 - 1]) * terms[n - 2][c, b, :, cols(j)]
                    terms[n][c, b, :, cols(j)] = value
                here, here_up = below, below_up

    for n in range(1, TERMS):
        for c in range(4):
            one_pass(n, c)


def combine(layout, scales, omega, slow_ref, terms, next_ref, maps_ref, beyond):
    order = Order(layout)
    start, stop = (layout.own, layout.out_blocks) if beyond else (0, layout.own)

    def one_block(b, carry):
        at = order.other(b) if beyond else order.own(b)
        for j in range(layout.columns):
            product = order.flip(slow_ref[j, layout.depth, rows_at(at), :]) * omega
            u = product * product * (2.0 / LARGEST**2) - 1.0
            sums = [None] * 4
            for n in range(TERMS):
                value = u * POLYNOMIALS[n][DEGREE] + POLYNOMIALS[n][DEGREE - 1]
                for k in range(DEGREE - 2, -1, -1):
                    value = value * u + POLYNOMIALS[n][k]
                if n % 2 == 1:
                    value = value * product
                for c in range(4):
                    if n % 2 == 0:
                        part = value * terms[n][c, b, :, cols(j)]
                        sums[c] = part if n == 0 else sums[c] + part
                    else:
                        part = value * terms[n][c ^ 1, b, :, cols(j)]
                        sums[c] = sums[c] - part if c in (0, 3) else sums[c] + part
            if next_ref is not None:
                for c in range(4):
                    next_ref[c, b, :, cols(j)] = sums[c]
            if not beyond:
                s_re, s_im, r_re, r_im = sums
                image = (s_re * r_re + s_im * r_im) * scales[0]
                energy = (s_re * s_re + s_im * s_im) * scales[1]
                maps_ref[rows_at(at), cols(j)] = order.flip(image)
                maps_ref[rows_at(layout.own + at), cols(j)] = order.flip(energy)
        return carry

    lax.fori_loop(start, stop, one_block, None)


VMEM = pl.BlockSpec(memory_space=pltpu.VMEM)
SMEM = pl.BlockSpec(memory_space=pltpu.SMEM)


def cost(flops):
    return pl.CostEstimate(flops=flops, bytes_accessed=2**20, transcendentals=0)


def first_terms(layout, source, receiver, other_source, other_receiver):
    def body(*refs):
        given, terms = refs[:4], refs[4:]
        order = Order(layout)
        for b in range(layout.blocks(0)):
            near = b < layout.own
            at = order.own(b) if near else order.other(b)
            for c in range(4):
                field = given[c // 2 + (0 if near else 2)]
                for j in range(layout.columns):
                    terms[0][c, b, :, cols(j)] = order.flip(field[c % 2, 0, rows_at(at), cols(j)])
        recursion(layout, terms)

    return pl.pallas_call(
        body,
        out_shape=[jax.ShapeDtypeStruct(layout.state(n), jnp.float32) for n in range(TERMS)],
        in_specs=[VMEM] * 4,
        out_specs=[VMEM] * TERMS,
        compiler_params=pltpu.CompilerParams(vmem_limit_bytes=16 * 2**20),
        cost_estimate=cost(8 * 10**9),
        name="first_terms",
    )(source, receiver, other_source, other_receiver)


def state(blocks, width):
    return jax.ShapeDtypeStruct((4, blocks, ROWS, width), jnp.float32)


def maps_shape(layout):
    return jax.ShapeDtypeStruct((2 * layout.own * ROWS, layout.width), jnp.float32)


def first_depth(layout, scales, omegas, terms, slow, other_slow):
    def body(omega_ref, slow_ref, other_ref, *refs):
        terms, maps_ref, next_ref = refs[:TERMS], refs[TERMS], refs[TERMS + 1]
        combine(layout, scales, omega_ref[0], slow_ref, terms, next_ref, maps_ref, False)
        combine(layout, scales, omega_ref[0], other_ref, terms, next_ref, None, True)

    return pl.pallas_call(
        body,
        out_shape=[maps_shape(layout), state(layout.out_blocks, layout.width)],
        in_specs=[SMEM] + [VMEM] * (2 + TERMS),
        out_specs=[VMEM] * 2,
        compiler_params=pltpu.CompilerParams(vmem_limit_bytes=16 * 2**20),
        cost_estimate=cost(3 * 10**9),
        name="first_depth",
    )(omegas, slow, other_slow, *terms)


def later_depth(layout, scales, omegas, fields, slow, other_slow):
    reaches = not layout.last

    def body(omega_ref, *refs):
        refs = list(refs)
        slow_ref = refs.pop(0)
        other_ref = refs.pop(0) if reaches else None
        fields_ref = refs.pop(0)
        maps_ref = refs.pop(0)
        next_ref = refs.pop(0) if reaches else None
        terms = [fields_ref] + refs
        recursion(layout, terms)
        combine(layout, scales, omega_ref[0], slow_ref, terms, next_ref, maps_ref, False)
        if reaches:
            combine(layout, scales, omega_ref[0], other_ref, terms, next_ref, None, True)

    out_shape = [maps_shape(layout)] + ([state(layout.out_blocks, layout.width)] if reaches else [])
    operands = [omegas, slow] + ([other_slow] if reaches else []) + [fields]
    return pl.pallas_call(
        body,
        out_shape=out_shape,
        in_specs=[SMEM] + [VMEM] * (len(operands) - 1),
        out_specs=[VMEM] * len(out_shape),
        scratch_shapes=[pltpu.VMEM(layout.state(n), jnp.float32) for n in range(1, TERMS)],
        compiler_params=pltpu.CompilerParams(vmem_limit_bytes=16 * 2**20),
        cost_estimate=cost(6 * 10**9),
        name="later_depth",
    )(*operands)


def gather(shard, axis):
    count = lax.axis_size(axis)
    return lax.all_to_all(jnp.broadcast_to(shard[None], (count,) + shard.shape), axis, 0, 0)


ANY = pl.BlockSpec(memory_space=pl.ANY)


def assemble(summed, tile_rows, width):
    count, steps, chunk = summed.shape[:3]
    direct = chunk % ROWS == 0

    def body(summed_ref, image_ref, energy_ref, staged, sems):
        copies = []

        def copy(piece, depth, at):
            out_ref, at = (image_ref, at) if at < tile_rows else (energy_ref, at - tile_rows)
            target = out_ref.at[depth, pl.ds(at, piece.shape[0])]
            copies.append(pltpu.make_async_copy(piece, target, sems.at[len(copies)]))
            copies[-1].start()

        for depth in range(steps):
            if direct:
                for source in range(count):
                    copy(summed_ref.at[source, depth], depth, source * chunk)
            else:
                for source in range(count):
                    staged[depth, source * chunk : (source + 1) * chunk] = summed_ref[source, depth]
                for at in (0, tile_rows):
                    copy(staged.at[depth, pl.ds(at, tile_rows)], depth, at)
        for each in copies:
            each.wait()

    shape = jax.ShapeDtypeStruct((steps, tile_rows, width), jnp.float32)
    return pl.pallas_call(
        body,
        out_shape=[shape, shape],
        in_specs=[ANY if direct else VMEM],
        out_specs=[ANY] * 2,
        scratch_shapes=[
            pltpu.VMEM((steps, 2 * tile_rows, width), jnp.float32),
            pltpu.SemaphoreType.DMA((steps * count,)),
        ],
        compiler_params=pltpu.CompilerParams(vmem_limit_bytes=8 * 2**20),
        cost_estimate=cost(10**8),
        name="assemble",
    )(summed)


def per_device(source_field, receiver_field, slowness, omegas):
    tiles = lax.axis_size("tile")
    assert tiles == 2
    swap = [(0, 1), (1, 0)]
    freqs = lax.axis_size("freq")
    tile_rows, width = source_field.shape[2], source_field.shape[3]
    scales = (1.0 / math.sqrt(omegas.shape[0] * freqs), 1.0 / (omegas.shape[0] * freqs))
    layouts = [Layout(depth, tile_rows, width) for depth in range(STEPS)]

    other_source = lax.ppermute(source_field, "tile", swap)
    other_receiver = lax.ppermute(receiver_field, "tile", swap)
    slow = gather(slowness, "freq")
    terms = first_terms(layouts[0], source_field, receiver_field, other_source, other_receiver)
    if slow.shape[-1] != LANES:
        slow = jnp.moveaxis(slow, 0, 2).reshape(STEPS, tile_rows, width // LANES, LANES)
        slow = jnp.moveaxis(slow, 2, 0)
    other_slow = lax.ppermute(slow, "tile", swap)

    chunk = 2 * tile_rows // freqs
    maps, fields = first_depth(layouts[0], scales, omegas, terms, slow, other_slow)
    every = [maps]
    for depth in range(1, STEPS):
        maps, *rest = later_depth(layouts[depth], scales, omegas, fields, slow, other_slow)
        fields = rest[0] if rest else None
        every.append(maps)
    parts = jnp.stack([maps.reshape(freqs, chunk, width) for maps in every], 1)
    reduced = jnp.sum(lax.all_to_all(parts, "freq", 0, 0), axis=0)
    return tuple(assemble(gather(reduced, "freq"), tile_rows, width))


def solution(mesh):
    in_specs = (
        P("shot", "freq", "tile", None),
        P("shot", "freq", "tile", None),
        P(None, "tile", "freq"),
        P("freq"),
    )
    out_specs = (P("shot", "tile", None), P("shot", "tile", None))
    return jax.shard_map(
        per_device, mesh=mesh, in_specs=in_specs, out_specs=out_specs, check_vma=False
    )
```

profile of v0, /device:TPU:0, one launch (start us, length us, event | category | flops | bytes accessed | tf_op | source)
XLA Modules:
  0.0 88.4 jit_solution(1138327274634486096)
XLA Ops:
  0.6 1.6 %broadcast_in_dim.4 = f32[8,3,32,128]{3,2,1,0:T(8,128)} broadcast(f32[3,32,128]{2,1,0:T(8,128)} %param.6), dimensions={1,2,3} | broadcast | bytes 442368 | tf_op jit(solution)/shard_map/broadcast_in_dim | solution.py:316
  2.2 0.0 copy-start
  2.2 0.0 copy-start.1
  2.2 7.4 %all-to-all-start = ((f32[8,3,32,128]{3,2,1,0:T(8,128)}), f32[8,3,32,128]{3,2,1,0:T(8,128)S(1)}, u32[]{:S(2)}, u32[]{:S(2)}) async-start(f32[8,3,32,128]{3,2,1,0:T(8,128)} %broadcast_in_dim.4), calls=%async_computation | async-start | bytes 786432 | tf_op jit(solution)/shard_map/all_to_all | solution.py:316
  9.6 0.0 copy-done
  9.6 0.1 collective-permute-start.1
  9.7 0.0 copy-done.1
  9.7 0.5 collective-permute-start.2
  10.9 10.5 %all-to-all-done.slow_ref.refs_0_ = f32[8,3,32,128]{3,2,1,0:T(8,128)S(1)} async-done(((f32[8,3,32,128]{3,2,1,0:T(8,128)}), f32[8,3,32,128]{3,2,1,0:T(8,128)S(1)}, u32[]{:S(2)}, u32[]{:S(2)}) %all-to-all-start) | async-done | bytes 393248 | tf_op jit(solution)/shard_map/all_to_all | solution.py:316
  21.3 0.0 collective-permute-start
  21.3 0.0 collective-permute-done.1.refs_2_
  21.3 0.0 collective-permute-done.2.refs_3_
  21.3 4.7 %first_terms.1 = (f32[4,8,8,1024]{3,2,1,0:T(8,128)S(1)}, f32[4,8,8,1024]{3,2,1,0:T(8,128)S(1)}, f32[4,8,8,1024]{3,2,1,0:T(8,128)S(1)}, f32[4,7,8,1024]{3,2,1,0:T...) custom-call(f32[2,1,32,1024]{3,2,1,0:T(8,128)S(1)} %copy-done, ...), custom_call_target="tpu_custom_call" | custom-call | flops 8000000000 | bytes 1048576 | tf_op jit(solution)/shard_map/first_terms/pallas_call | solution.py:248
  26.0 0.0 collective-permute-done.other_ref.refs_1_
  26.0 2.4 %first_depth.1 = (f32[64,1024]{1,0:T(8,128)S(1)}, f32[4,7,8,1024]{3,2,1,0:T(8,128)S(1)}) custom-call(f32[1]{0:T(128)S(6)} %copy.9.omega_ref, f32[8,3,32,128]{3,2,1,0:T(8,128)S(1)} %all-to-all-done.slow_ref.refs_0_, f32[8,3,32,128]{3,2,1,0:T(8,128)S(1)} %collective-permute-done.other_ref.refs_1_, f32[4,8,8,1024]{3,2,1,0:T(8,128)S(1)} %get-tuple-element.16.refs_0_, ...), custom_call_target="tpu_custom_call" | custom-call | flops 3000000000 | bytes 1048576 | tf_op jit(solution)/shard_map/first_depth/pallas_call | solution.py:273
  28.4 6.1 %later_depth.2 = (f32[64,1024]{1,0:T(8,128)S(1)}, f32[4,6,8,1024]{3,2,1,0:T(8,128)S(1)}) custom-call(f32[1]{0:T(128)S(6)} %copy.9.omega_ref, f32[8,3,32,128]{3,2,1,0:T(8,128)S(1)} %all-to-all-done.slow_ref.refs_0_, f32[8,3,32,128]{3,2,1,0:T(8,128)S(1)} %collective-permute-done.other_ref.refs_1_, f32[4,7,8,1024]{3,2,1,0:T(8,128)S(1)} %get-tuple-element.27.refs_2_), custom_call_target="tpu_custom_call" | custom-call | flops 6000000000 | bytes 1048576 | tf_op jit(solution)/shard_map/later_depth/pallas_call | solution.py:302
  34.5 4.5 %later_depth.3 = f32[64,1024]{1,0:T(8,128)S(1)} custom-call(f32[1]{0:T(128)S(6)} %copy.9.omega_ref, f32[8,3,32,128]{3,2,1,0:T(8,128)S(1)} %all-to-all-done.slow_ref.refs_0_, f32[4,6,8,1024]{3,2,1,0:T(8,128)S(1)} %get-tuple-element.29.refs_1_), custom_call_target="tpu_custom_call" | custom-call | flops 6000000000 | bytes 1048576 | tf_op jit(solution)/shard_map/later_depth/pallas_call | solution.py:302
  39.0 0.1 pad_maximum_fusion
  39.1 24.2 %all_to_all.15 = f32[8,3,8,1024]{3,2,1,0:T(8,128)S(1)} all-to-all(f32[8,3,8,1024]{3,2,1,0:T(8,128)S(1)} %pad_maximum_fusion), channel_id=1, replica_groups=mesh['shot'=2,'freq'=8,'tile'=2] {'freq'}, dimensions={0} | all-to-all | bytes 1572864 | tf_op jit(solution)/shard_map/all_to_all | solution.py:389
  63.3 0.1 broadcast_in_dim.5
  63.4 23.7 %all_to_all.16.summed_ref = f32[8,3,8,1024]{3,2,1,0:T(8,128)S(1)} all-to-all(f32[8,3,8,1024]{3,2,1,0:T(8,128)S(1)} %broadcast_in_dim.5), channel_id=1, replica_groups=mesh['shot'=2,'freq'=8,'tile'=2] {'freq'}, dimensions={0} | all-to-all | bytes 1572864 | tf_op jit(solution)/shard_map/all_to_all | solution.py:316
  87.1 1.1 %assemble.1 = (f32[3,32,1024]{2,1,0:T(8,128)}, f32[3,32,1024]{2,1,0:T(8,128)}) custom-call(f32[8,3,8,1024]{3,2,1,0:T(8,128)S(1)} %all_to_all.16.summed_ref), custom_call_target="tpu_custom_call" | custom-call | flops 100000000 | bytes 1048576 | tf_op jit(solution)/shard_map/assemble/pallas_call | solution.py:348
  (1 shorter events, 0.0 us)
Async XLA Ops:
  2.2 7.4 %copy-start = (f32[2,1,32,1024]{3,2,1,0:T(8,128)S(1)}, f32[2,1,32,1024]{3,2,1,0:T(8,128)}, u32[]{:S(2)}) copy-start(f32[2,1,32,1024]{3,2,1,0:T(8,128)} %refs_0_.1) | copy-start | bytes 786436
  2.2 7.5 %copy-start.1 = (f32[2,1,32,1024]{3,2,1,0:T(8,128)S(1)}, f32[2,1,32,1024]{3,2,1,0:T(8,128)}, u32[]{:S(2)}) copy-start(f32[2,1,32,1024]{3,2,1,0:T(8,128)} %refs_1_.1) | copy-start | bytes 786436
  2.2 19.1 %all-to-all-start = ((f32[8,3,32,128]{3,2,1,0:T(8,128)}), f32[8,3,32,128]{3,2,1,0:T(8,128)S(1)}, u32[]{:S(2)}, u32[]{:S(2)}) async-start(f32[8,3,32,128]{3,2,1,0:T(8,128)} %broadcast_in_dim.4), calls=%async_computation | async-start | bytes 786432 | tf_op jit(solution)/shard_map/all_to_all | solution.py:316
  9.6 11.7 %collective-permute-start.1 = (f32[2,1,32,1024]{3,2,1,0:T(8,128)S(1)}, f32[2,1,32,1024]{3,2,1,0:T(8,128)S(1)}, u32[]{:S(2)}, u32[]{:S(2)}) collective-permute-start(f32[2,1,32,1024]{3,2,1,0:T(8,128)S(1)} %copy-done), channel_id=1, source_target_pairs={{0,1},{1,0},{2,3},{3,2},{4,5},{5,4},{6,7},{7,6},{8,9},{9,8},{10,11... | collective-permute-start | bytes 786440 | tf_op jit(solution)/shard_map/ppermute | solution.py:372
  9.7 11.6 %collective-permute-start.2 = (f32[2,1,32,1024]{3,2,1,0:T(8,128)S(1)}, f32[2,1,32,1024]{3,2,1,0:T(8,128)S(1)}, u32[]{:S(2)}, u32[]{:S(2)}) collective-permute-start(f32[2,1,32,1024]{3,2,1,0:T(8,128)S(1)} %copy-done.1), channel_id=1, source_target_pairs={{0,1},{1,0},{2,3},{3,2},{4,5},{5,4},{6,7},{7,6},{8,9},{9,8},{10,11... | collective-permute-start | bytes 786440 | tf_op jit(solution)/shard_map/ppermute | solution.py:373
  21.3 4.7 %collective-permute-start = (f32[8,3,32,128]{3,2,1,0:T(8,128)S(1)}, f32[8,3,32,128]{3,2,1,0:T(8,128)S(1)}, u32[]{:S(2)}, u32[]{:S(2)}) collective-permute-start(f32[8,3,32,128]{3,2,1,0:T(8,128)S(1)} %all-to-all-done.slow_ref.refs_0_), channel_id=1, source_target_pairs={{0,1},{1,0},{2,3},{3,2},{4,5},{5,4},{6,7},{7,6},{8,9},{9,8},{10,11... | collective-permute-start | bytes 1179656 | tf_op jit(solution)/shard_map/ppermute | solution.py:379
where the time goes:
time: 88.7 us; the launch traced here: 88.4 us
  blocking collectives  47.9 us (54%)
  Pallas kernels  18.7 us (21%)
  waiting for transfers between devices  10.5 us (12%)
  starting transfers between devices  7.98 us (9%)
  local copies, waits for them, and re-layouts  1.67 us (2%)
  between operations  1.52 us (2%)
    all_to_all x1, blocking collectives, per_device(): reduced = jnp.sum(lax.all_to_all(parts, 'freq', 0, 0), axis=0)  24.2 us
    all_to_all x1, blocking collectives, gather(): lax.all_to_all(jnp.broadcast_to(shard[None], (count,) + shard.shape), axi...  23.7 us
    pallas_call x2, Pallas kernels, later_depth(): pl.pallas_call(body, out_shape=out_shape, in_specs=[SMEM] + [VMEM] * (len...  10.5 us
    all_to_all x1, waiting for transfers between devices, gather(): lax.all_to_all(jnp.broadcast_to(shard[None], (count,) + shard.shape), axi...  10.5 us
    all_to_all x1, starting transfers between devices, gather(): lax.all_to_all(jnp.broadcast_to(shard[None], (count,) + shard.shape), axi...  7.41 us
    pallas_call x1, Pallas kernels, first_terms(): pl.pallas_call(body, out_shape=[jax.ShapeDtypeStruct(layout.state(n), jnp...  4.65 us
    pallas_call x1, Pallas kernels, first_depth(): pl.pallas_call(body, out_shape=[maps_shape(layout), state(layout.out_bloc...  2.43 us
  transfers between devices with their start and end apart: 4, of which 1 were waited for; matrix products, arithmetic and copies ran while one was open for 0% of the time, Pallas kernels for 5%

commit v1 on v0

--- a/solution.py
+++ b/solution.py
@@ -319,28 +319,59 @@
 ANY = pl.BlockSpec(memory_space=pl.ANY)
 
 
-def assemble(summed, tile_rows, width):
-    count, steps, chunk = summed.shape[:3]
+def halves(count):
+    half = count // 2
+    groups = [list(range(half)), list(range(half, count))]
+    return half, groups, [(i, (i + half) % count) for i in range(count)]
+
+
+def reduce_rows(maps, axis):
+    half, groups, between = halves(lax.axis_size(axis))
+    parts = lax.all_to_all(maps, axis, 0, 0, axis_index_groups=groups)
+    summed = jnp.sum(parts, axis=0)
+    upper = lax.axis_index(axis) >= half
+    mine = jnp.where(upper, summed[1], summed[0])
+    theirs = jnp.where(upper, summed[0], summed[1])
+    return mine + lax.ppermute(theirs, axis, between)
+
+
+def gather_rows(rows, axis):
+    half, groups, between = halves(lax.axis_size(axis))
+    pair = jnp.stack([rows, lax.ppermute(rows, axis, between)])
+    return lax.all_to_all(
+        jnp.broadcast_to(pair[None], (half,) + pair.shape), axis, 0, 0, axis_index_groups=groups
+    )
+
+
+def assemble(gathered, tile_rows, width):
+    half, _, steps, chunk = gathered.shape[:4]
     direct = chunk % ROWS == 0
 
-    def body(summed_ref, image_ref, energy_ref, staged, sems):
+    def body(gathered_ref, image_ref, energy_ref, staged, sems):
+        upper = (lax.axis_index("freq") >= half).astype(jnp.int32)
         copies = []
 
-        def copy(piece, depth, at):
-            out_ref, at = (image_ref, at) if at < tile_rows else (energy_ref, at - tile_rows)
-            target = out_ref.at[depth, pl.ds(at, piece.shape[0])]
+        def copy(piece, depth, start, offset):
+            out_ref, start = (image_ref, start) if start < tile_rows else (energy_ref, start - tile_rows)
+            target = out_ref.at[depth, pl.ds(start + offset, piece.shape[0])]
             copies.append(pltpu.make_async_copy(piece, target, sems.at[len(copies)]))
             copies[-1].start()
 
         for depth in range(steps):
             if direct:
-                for source in range(count):
-                    copy(summed_ref.at[source, depth], depth, source * chunk)
+                for p in range(half):
+                    for k in range(2):
+                        offset = pl.multiple_of((upper ^ k) * chunk, chunk)
+                        copy(gathered_ref.at[p, k, depth], depth, 2 * p * chunk, offset)
             else:
-                for source in range(count):
-                    staged[depth, source * chunk : (source + 1) * chunk] = summed_ref[source, depth]
-                for at in (0, tile_rows):
-                    copy(staged.at[depth, pl.ds(at, tile_rows)], depth, at)
+                for p in range(half):
+                    for k in range(2):
+                        start = (2 * p + k) * chunk
+                        staged[depth, start : start + chunk] = jnp.where(
+                            upper == 0, gathered_ref[p, k, depth], gathered_ref[p, 1 - k, depth]
+                        )
+                for start in (0, tile_rows):
+                    copy(staged.at[depth, pl.ds(start, tile_rows)], depth, start, 0)
         for each in copies:
             each.wait()
 
@@ -352,12 +383,12 @@
         out_specs=[ANY] * 2,
         scratch_shapes=[
             pltpu.VMEM((steps, 2 * tile_rows, width), jnp.float32),
-            pltpu.SemaphoreType.DMA((steps * count,)),
+            pltpu.SemaphoreType.DMA((steps * 2 * half,)),
         ],
         compiler_params=pltpu.CompilerParams(vmem_limit_bytes=8 * 2**20),
         cost_estimate=cost(10**8),
         name="assemble",
-    )(summed)
+    )(gathered)
 
 
 def per_device(source_field, receiver_field, slowness, omegas):
@@ -385,9 +416,8 @@
         maps, *rest = later_depth(layouts[depth], scales, omegas, fields, slow, other_slow)
         fields = rest[0] if rest else None
         every.append(maps)
-    parts = jnp.stack([maps.reshape(freqs, chunk, width) for maps in every], 1)
-    reduced = jnp.sum(lax.all_to_all(parts, "freq", 0, 0), axis=0)
-    return tuple(assemble(gather(reduced, "freq"), tile_rows, width))
+    parts = jnp.stack([maps.reshape(freqs // 2, 2, chunk, width) for maps in every], 2)
+    return tuple(assemble(gather_rows(reduce_rows(parts, "freq"), "freq"), tile_rows, width))
 
 
 def solution(mesh):

time: 88.7 us -> 83.5 us (0.941)
  blocking collectives: 47.9 us -> 13.2 us
  waiting for transfers between devices: 10.5 us -> 34.6 us
  starting transfers between devices: 7.98 us -> 12.4 us
  other arithmetic: 0.11 us -> 1.07 us
    all_to_all x2 -> x1, blocking collectives: 47.9 us -> 13.2 us  [gather_rows(): lax.all_to_all(jnp.broadcast_to(pair[None], (half,) + pair.shape), axis,...]
    ppermute x0 -> x2, waiting for transfers between devices: none -> 12.4 us  [the longest x1 6.76 us: reduce_rows(): return mine + lax.ppermute(theirs, axis, between)]
    all_to_all x0 -> x1, waiting for transfers between devices: none -> 11.7 us  [reduce_rows(): parts = lax.all_to_all(maps, axis, 0, 0, axis_index_groups=groups)]
    all_to_all x0 -> x1, starting transfers between devices: none -> 3.49 us  [reduce_rows(): parts = lax.all_to_all(maps, axis, 0, 0, axis_index_groups=groups)]
    ppermute x0 -> x2, starting transfers between devices: none -> 0.94 us  [the longest x1 0.87 us: reduce_rows(): return mine + lax.ppermute(theirs, axis, between)]
    another operation x1 -> x2, other arithmetic: 0.07 us -> 0.98 us  [the longest x1 0.97 us: per_device(): jnp.stack([maps.reshape(freqs // 2, 2, chunk, width) for maps in every], 2)]
  transfers between devices with their start and end apart: 4 -> 7, of which waited for: 1 -> 4; matrix products, arithmetic and copies ran while one was open for 0% -> 0% of each run, Pallas kernels for 5% -> 6%
where the time goes in v1:
time: 83.5 us; the launch traced here: 83.2 us
  waiting for transfers between devices  34.6 us (41%)
  Pallas kernels  18.7 us (22%)
  blocking collectives  13.2 us (16%)
  starting transfers between devices  12.4 us (15%)
  local copies, waits for them, and re-layouts  1.67 us (2%)
  between operations  1.55 us (2%)
  other arithmetic  1.07 us (1%)
    all_to_all x1, blocking collectives, gather_rows(): lax.all_to_all(jnp.broadcast_to(pair[None], (half,) + pair.shape), axis,...  13.2 us
    all_to_all x1, waiting for transfers between devices, reduce_rows(): parts = lax.all_to_all(maps, axis, 0, 0, axis_index_groups=groups)  11.7 us
    pallas_call x2, Pallas kernels, later_depth(): pl.pallas_call(body, out_shape=out_shape, in_specs=[SMEM] + [VMEM] * (len...  10.5 us
    all_to_all x1, waiting for transfers between devices, gather(): lax.all_to_all(jnp.broadcast_to(shard[None], (count,) + shard.shape), axi...  10.5 us
    all_to_all x1, starting transfers between devices, gather(): lax.all_to_all(jnp.broadcast_to(shard[None], (count,) + shard.shape), axi...  7.41 us
    ppermute x1, waiting for transfers between devices, reduce_rows(): return mine + lax.ppermute(theirs, axis, between)  6.76 us
    ppermute x1, waiting for transfers between devices, gather_rows(): pair = jnp.stack([rows, lax.ppermute(rows, axis, between)])  5.6 us
    pallas_call x1, Pallas kernels, first_terms(): pl.pallas_call(body, out_shape=[jax.ShapeDtypeStruct(layout.state(n), jnp...  4.65 us
  transfers between devices with their start and end apart: 7, of which 4 were waited for; matrix products, arithmetic and copies ran while one was open for 0% of the time, Pallas kernels for 6%

profile of v1, /device:TPU:0, one launch (start us, length us, event | category | flops | bytes accessed | tf_op | source)
XLA Modules:
  0.0 83.2 jit_solution(14330392002732882825)
XLA Ops:
  0.6 1.6 %broadcast_in_dim.4 = f32[8,3,32,128]{3,2,1,0:T(8,128)} broadcast(f32[3,32,128]{2,1,0:T(8,128)} %param.6), dimensions={1,2,3} | broadcast | bytes 442368 | tf_op jit(solution)/shard_map/broadcast_in_dim | solution.py:316
  2.2 0.0 copy-start
  2.2 0.0 copy-start.1
  2.2 7.4 %all-to-all-start = ((f32[8,3,32,128]{3,2,1,0:T(8,128)}), f32[8,3,32,128]{3,2,1,0:T(8,128)S(1)}, u32[]{:S(2)}, u32[]{:S(2)}) async-start(f32[8,3,32,128]{3,2,1,0:T(8,128)} %broadcast_in_dim.4), calls=%async_computation | async-start | bytes 786432 | tf_op jit(solution)/shard_map/all_to_all | solution.py:316
  9.6 0.0 copy-done
  9.6 0.1 collective-permute-start.1
  9.7 0.0 copy-done.1
  9.7 0.5 collective-permute-start.2
  10.9 10.5 %all-to-all-done.slow_ref.refs_0_ = f32[8,3,32,128]{3,2,1,0:T(8,128)S(1)} async-done(((f32[8,3,32,128]{3,2,1,0:T(8,128)}), f32[8,3,32,128]{3,2,1,0:T(8,128)S(1)}, u32[]{:S(2)}, u32[]{:S(2)}) %all-to-all-start) | async-done | bytes 393248 | tf_op jit(solution)/shard_map/all_to_all | solution.py:316
  21.3 0.0 collective-permute-start
  21.3 0.0 collective-permute-done.1.refs_2_
  21.3 0.0 collective-permute-done.2.refs_3_
  21.3 4.7 %first_terms.1 = (f32[4,8,8,1024]{3,2,1,0:T(8,128)S(1)}, f32[4,8,8,1024]{3,2,1,0:T(8,128)S(1)}, f32[4,8,8,1024]{3,2,1,0:T(8,128)S(1)}, f32[4,7,8,1024]{3,2,1,0:T...) custom-call(f32[2,1,32,1024]{3,2,1,0:T(8,128)S(1)} %copy-done, ...), custom_call_target="tpu_custom_call" | custom-call | flops 8000000000 | bytes 1048576 | tf_op jit(solution)/shard_map/first_terms/pallas_call | solution.py:248
  26.0 0.0 collective-permute-done.other_ref.refs_1_
  26.0 2.4 %first_depth.1 = (f32[64,1024]{1,0:T(8,128)S(1)}, f32[4,7,8,1024]{3,2,1,0:T(8,128)S(1)}) custom-call(f32[1]{0:T(128)S(6)} %copy.16.omega_ref, f32[8,3,32,128]{3,2,1,0:T(8,128)S(1)} %all-to-all-done.slow_ref.refs_0_, f32[8,3,32,128]{3,2,1,0:T(8,128)S(1)} %collective-permute-done.other_ref.refs_1_, f32[4,8,8,1024]{3,2,1,0:T(8,128)S(1)} %get-tuple-element.16.refs_0_, ...), custom_call_target="tpu_custom_call" | custom-call | flops 3000000000 | bytes 1048576 | tf_op jit(solution)/shard_map/first_depth/pallas_call | solution.py:273
  28.4 6.1 %later_depth.2 = (f32[64,1024]{1,0:T(8,128)S(1)}, f32[4,6,8,1024]{3,2,1,0:T(8,128)S(1)}) custom-call(f32[1]{0:T(128)S(6)} %copy.16.omega_ref, f32[8,3,32,128]{3,2,1,0:T(8,128)S(1)} %all-to-all-done.slow_ref.refs_0_, f32[8,3,32,128]{3,2,1,0:T(8,128)S(1)} %collective-permute-done.other_ref.refs_1_, f32[4,7,8,1024]{3,2,1,0:T(8,128)S(1)} %get-tuple-element.27.refs_2_), custom_call_target="tpu_custom_call" | custom-call | flops 6000000000 | bytes 1048576 | tf_op jit(solution)/shard_map/later_depth/pallas_call | solution.py:302
  34.5 4.5 %later_depth.3 = f32[64,1024]{1,0:T(8,128)S(1)} custom-call(f32[1]{0:T(128)S(6)} %copy.16.omega_ref, f32[8,3,32,128]{3,2,1,0:T(8,128)S(1)} %all-to-all-done.slow_ref.refs_0_, f32[4,6,8,1024]{3,2,1,0:T(8,128)S(1)} %get-tuple-element.29.refs_1_), custom_call_target="tpu_custom_call" | custom-call | flops 6000000000 | bytes 1048576 | tf_op jit(solution)/shard_map/later_depth/pallas_call | solution.py:302
  39.0 1.0 %pad_maximum_fusion = f32[4,2,3,8,1024]{4,3,1,2,0:T(8,128)} fusion(f32[4,2,1,8,1024]{4,3,1,2,0:T(8,128)S(1)} %bitcast.31, f32[4,2,1,8,1024]{4,3,1,2,0:T(8,128)S(1)} %bitcast.30, f32[4,2,1,8,1024]{4,3,1,2,0:T(8,128)S(1)} %bitcast.29), kind=kLoop, calls=%fused_computation | loop fusion | flops 393216 | bytes 1572864 | tf_op jit(solution)/shard_map/stack | solution.py:419
  40.0 3.5 %all-to-all-start.1 = ((f32[4,2,3,8,1024]{4,3,1,2,0:T(8,128)}), f32[4,2,3,8,1024]{4,3,1,2,0:T(8,128)S(1)}, u32[]{:S(2)}, u32[]{:S(2)}) async-start(f32[4,2,3,8,1024]{4,3,1,2,0:T(8,128)} %pad_maximum_fusion), calls=%async_computation.1 | async-start | bytes 1572864 | tf_op jit(solution)/shard_map/all_to_all | solution.py:330
  43.5 11.7 %all-to-all-done.1 = f32[4,2,3,8,1024]{4,3,1,2,0:T(8,128)S(1)} async-done(((f32[4,2,3,8,1024]{4,3,1,2,0:T(8,128)}), f32[4,2,3,8,1024]{4,3,1,2,0:T(8,128)S(1)}, u32[]{:S(2)}, u32[]{:S(2)}) %all-to-all-start.1) | async-done | bytes 786464 | tf_op jit(solution)/shard_map/all_to_all | solution.py:330
  55.3 0.9 %collective-permute-start.3 = (f32[3,8,1024]{2,1,0:T(8,128)S(1)}, f32[3,8,1024]{2,1,0:T(8,128)S(1)}, u32[]{:S(2)}, u32[]{:S(2)}) collective-permute-start(f32[3,8,1024]{2,1,0:T(8,128)S(1)} %select_bitcast_fusion), channel_id=1, source_target_pairs={{0,8},{2,10},{4,12},{6,14},{8,0},{10,2},{12,4},{14,6},{1,9},{3,11}... | collective-permute-start | bytes 294920 | tf_op jit(solution)/shard_map/ppermute | solution.py:335
  56.1 6.8 %collective-permute-done.3 = f32[3,8,1024]{2,1,0:T(8,128)S(1)} collective-permute-done((f32[3,8,1024]{2,1,0:T(8,128)S(1)}, f32[3,8,1024]{2,1,0:T(8,128)S(1)}, u32[]{:S(2)}, u32[]{:S(2)}) %collective-permute-start.3) | collective-permute-done | bytes 98336 | tf_op jit(solution)/shard_map/ppermute | solution.py:335
  62.9 0.1 collective-permute-start.4
  63.0 5.6 %collective-permute-done.4 = f32[3,8,1024]{2,1,0:T(8,128)S(1)} collective-permute-done((f32[3,8,1024]{2,1,0:T(8,128)S(1)}, f32[3,8,1024]{2,1,0:T(8,128)S(1)}, u32[]{:S(2)}, u32[]{:S(2)}) %collective-permute-start.4) | collective-permute-done | bytes 98336 | tf_op jit(solution)/shard_map/ppermute | solution.py:340
  68.6 0.1 broadcast_in_dim.5
  68.7 13.2 %all_to_all.15.gathered_ref = f32[4,2,3,8,1024]{4,3,2,1,0:T(8,128)S(1)} all-to-all(f32[4,2,3,8,1024]{4,3,2,1,0:T(8,128)S(1)} %broadcast_in_dim.5), channel_id=1, replica_groups={{0,2,4,6},{8,10,12,14},{1,3,5,7},{9,11,13,15},{16,18,20,22},{24,26,28,3..., dimensions={0} | all-to-all | bytes 1572864 | tf_op jit(solution)/shard_map/all_to_all | solution.py:341
  81.9 1.1 %assemble.1 = (f32[3,32,1024]{2,1,0:T(8,128)}, f32[3,32,1024]{2,1,0:T(8,128)}) custom-call(f32[4,2,3,8,1024]{4,3,2,1,0:T(8,128)S(1)} %all_to_all.15.gathered_ref), custom_call_target="tpu_custom_call" | custom-call | flops 100000000 | bytes 1048576 | tf_op jit(solution)/shard_map/assemble/pallas_call | solution.py:379
  (4 shorter events, 0.1 us)
Async XLA Ops:
  2.2 7.4 %copy-start = (f32[2,1,32,1024]{3,2,1,0:T(8,128)S(1)}, f32[2,1,32,1024]{3,2,1,0:T(8,128)}, u32[]{:S(2)}) copy-start(f32[2,1,32,1024]{3,2,1,0:T(8,128)} %refs_0_.1) | copy-start | bytes 786436
  2.2 7.5 %copy-start.1 = (f32[2,1,32,1024]{3,2,1,0:T(8,128)S(1)}, f32[2,1,32,1024]{3,2,1,0:T(8,128)}, u32[]{:S(2)}) copy-start(f32[2,1,32,1024]{3,2,1,0:T(8,128)} %refs_1_.1) | copy-start | bytes 786436
  2.2 19.1 %all-to-all-start = ((f32[8,3,32,128]{3,2,1,0:T(8,128)}), f32[8,3,32,128]{3,2,1,0:T(8,128)S(1)}, u32[]{:S(2)}, u32[]{:S(2)}) async-start(f32[8,3,32,128]{3,2,1,0:T(8,128)} %broadcast_in_dim.4), calls=%async_computation | async-start | bytes 786432 | tf_op jit(solution)/shard_map/all_to_all | solution.py:316
  9.6 11.7 %collective-permute-start.1 = (f32[2,1,32,1024]{3,2,1,0:T(8,128)S(1)}, f32[2,1,32,1024]{3,2,1,0:T(8,128)S(1)}, u32[]{:S(2)}, u32[]{:S(2)}) collective-permute-start(f32[2,1,32,1024]{3,2,1,0:T(8,128)S(1)} %copy-done), channel_id=1, source_target_pairs={{0,1},{1,0},{2,3},{3,2},{4,5},{5,4},{6,7},{7,6},{8,9},{9,8},{10,11... | collective-permute-start | bytes 786440 | tf_op jit(solution)/shard_map/ppermute | solution.py:403
  9.7 11.6 %collective-permute-start.2 = (f32[2,1,32,1024]{3,2,1,0:T(8,128)S(1)}, f32[2,1,32,1024]{3,2,1,0:T(8,128)S(1)}, u32[]{:S(2)}, u32[]{:S(2)}) collective-permute-start(f32[2,1,32,1024]{3,2,1,0:T(8,128)S(1)} %copy-done.1), channel_id=1, source_target_pairs={{0,1},{1,0},{2,3},{3,2},{4,5},{5,4},{6,7},{7,6},{8,9},{9,8},{10,11... | collective-permute-start | bytes 786440 | tf_op jit(solution)/shard_map/ppermute | solution.py:404
  21.3 4.7 %collective-permute-start = (f32[8,3,32,128]{3,2,1,0:T(8,128)S(1)}, f32[8,3,32,128]{3,2,1,0:T(8,128)S(1)}, u32[]{:S(2)}, u32[]{:S(2)}) collective-permute-start(f32[8,3,32,128]{3,2,1,0:T(8,128)S(1)} %all-to-all-done.slow_ref.refs_0_), channel_id=1, source_target_pairs={{0,1},{1,0},{2,3},{3,2},{4,5},{5,4},{6,7},{7,6},{8,9},{9,8},{10,11... | collective-permute-start | bytes 1179656 | tf_op jit(solution)/shard_map/ppermute | solution.py:410
  40.0 15.2 %all-to-all-start.1 = ((f32[4,2,3,8,1024]{4,3,1,2,0:T(8,128)}), f32[4,2,3,8,1024]{4,3,1,2,0:T(8,128)S(1)}, u32[]{:S(2)}, u32[]{:S(2)}) async-start(f32[4,2,3,8,1024]{4,3,1,2,0:T(8,128)} %pad_maximum_fusion), calls=%async_computation.1 | async-start | bytes 1572864 | tf_op jit(solution)/shard_map/all_to_all | solution.py:330
  55.3 7.6 %collective-permute-start.3 = (f32[3,8,1024]{2,1,0:T(8,128)S(1)}, f32[3,8,1024]{2,1,0:T(8,128)S(1)}, u32[]{:S(2)}, u32[]{:S(2)}) collective-permute-start(f32[3,8,1024]{2,1,0:T(8,128)S(1)} %select_bitcast_fusion), channel_id=1, source_target_pairs={{0,8},{2,10},{4,12},{6,14},{8,0},{10,2},{12,4},{14,6},{1,9},{3,11}... | collective-permute-start | bytes 294920 | tf_op jit(solution)/shard_map/ppermute | solution.py:335
  62.9 5.7 %collective-permute-start.4 = (f32[3,8,1024]{2,1,0:T(8,128)S(1)}, f32[3,8,1024]{2,1,0:T(8,128)S(1)}, u32[]{:S(2)}, u32[]{:S(2)}) collective-permute-start(f32[3,8,1024]{2,1,0:T(8,128)S(1)} %fusion.1), channel_id=1, source_target_pairs={{0,8},{2,10},{4,12},{6,14},{8,0},{10,2},{12,4},{14,6},{1,9},{3,11}... | collective-permute-start | bytes 294920 | tf_op jit(solution)/shard_map/ppermute | solution.py:340

commit v2 on v1

--- a/solution.py
+++ b/solution.py
@@ -189,12 +189,14 @@
 
 def combine(layout, scales, omega, slow_ref, terms, next_ref, maps_ref, beyond):
     order = Order(layout)
+    upper = in_upper_half("freq").astype(jnp.int32)
     start, stop = (layout.own, layout.out_blocks) if beyond else (0, layout.own)
 
     def one_block(b, carry):
         at = order.other(b) if beyond else order.own(b)
         for j in range(layout.columns):
-            product = order.flip(slow_ref[j, layout.depth, rows_at(at), :]) * omega
+            p, k = j % (layout.columns // 2), j // (layout.columns // 2)
+            product = order.flip(slow_ref[p, k ^ upper, layout.depth, rows_at(at), :]) * omega
             u = product * product * (2.0 / LARGEST**2) - 1.0
             sums = [None] * 4
             for n in range(TERMS):
@@ -226,6 +228,7 @@
 
 VMEM = pl.BlockSpec(memory_space=pltpu.VMEM)
 SMEM = pl.BlockSpec(memory_space=pltpu.SMEM)
+ANY = pl.BlockSpec(memory_space=pl.ANY)
 
 
 def cost(flops):
@@ -311,12 +314,19 @@
     )(*operands)
 
 
-def gather(shard, axis):
-    count = lax.axis_size(axis)
-    return lax.all_to_all(jnp.broadcast_to(shard[None], (count,) + shard.shape), axis, 0, 0)
-
-
-ANY = pl.BlockSpec(memory_space=pl.ANY)
+def in_upper_half(axis):
+    return lax.axis_index(axis) >= lax.axis_size(axis) // 2
+
+
+def all_slowness(slowness, width):
+    slow = gather_rows(slowness, "freq")
+    if slowness.shape[-1] == LANES:
+        return slow
+    upper = in_upper_half("freq")
+    slow = jnp.where(upper, slow[:, ::-1], slow)
+    slow = jnp.moveaxis(slow, (1, 0), (2, 3)).reshape(slowness.shape[:2] + (2, width // LANES // 2, LANES))
+    slow = jnp.moveaxis(slow, (3, 2), (0, 1))
+    return jnp.where(upper, slow[:, ::-1], slow)
 
 
 def halves(count):
@@ -325,22 +335,23 @@
     return half, groups, [(i, (i + half) % count) for i in range(count)]
 
 
-def reduce_rows(maps, axis):
+def sum_rows(maps, axis):
     half, groups, between = halves(lax.axis_size(axis))
-    parts = lax.all_to_all(maps, axis, 0, 0, axis_index_groups=groups)
+    flat = maps.reshape(half, -1, maps.shape[-1])
+    parts = lax.all_to_all(flat, axis, 0, 0, axis_index_groups=groups)
     summed = jnp.sum(parts, axis=0)
-    upper = lax.axis_index(axis) >= half
-    mine = jnp.where(upper, summed[1], summed[0])
-    theirs = jnp.where(upper, summed[0], summed[1])
-    return mine + lax.ppermute(theirs, axis, between)
+    summed = summed + lax.ppermute(summed, axis, between)
+    spread = jnp.broadcast_to(summed[None], (half,) + summed.shape)
+    return lax.all_to_all(spread, axis, 0, 0, axis_index_groups=groups).reshape(maps.shape)
 
 
 def gather_rows(rows, axis):
     half, groups, between = halves(lax.axis_size(axis))
-    pair = jnp.stack([rows, lax.ppermute(rows, axis, between)])
-    return lax.all_to_all(
-        jnp.broadcast_to(pair[None], (half,) + pair.shape), axis, 0, 0, axis_index_groups=groups
-    )
+    others = lax.ppermute(rows, axis, between)
+    own = lax.broadcasted_iota(jnp.int32, (half, 2) + (1,) * rows.ndim, 1) == 0
+    pairs = jnp.where(own, rows, others)
+    flat = pairs.reshape(half, -1, rows.shape[-1])
+    return lax.all_to_all(flat, axis, 0, 0, axis_index_groups=groups).reshape(pairs.shape)
 
 
 def assemble(gathered, tile_rows, width):
@@ -348,12 +359,11 @@
     direct = chunk % ROWS == 0
 
     def body(gathered_ref, image_ref, energy_ref, staged, sems):
-        upper = (lax.axis_index("freq") >= half).astype(jnp.int32)
         copies = []
 
-        def copy(piece, depth, start, offset):
+        def copy(piece, depth, start):
             out_ref, start = (image_ref, start) if start < tile_rows else (energy_ref, start - tile_rows)
-            target = out_ref.at[depth, pl.ds(start + offset, piece.shape[0])]
+            target = out_ref.at[depth, pl.ds(start, piece.shape[0])]
             copies.append(pltpu.make_async_copy(piece, target, sems.at[len(copies)]))
             copies[-1].start()
 
@@ -361,17 +371,14 @@
             if direct:
                 for p in range(half):
                     for k in range(2):
-                        offset = pl.multiple_of((upper ^ k) * chunk, chunk)
-                        copy(gathered_ref.at[p, k, depth], depth, 2 * p * chunk, offset)
+                        copy(gathered_ref.at[p, k, depth], depth, (2 * p + k) * chunk)
             else:
                 for p in range(half):
                     for k in range(2):
                         start = (2 * p + k) * chunk
-                        staged[depth, start : start + chunk] = jnp.where(
-                            upper == 0, gathered_ref[p, k, depth], gathered_ref[p, 1 - k, depth]
-                        )
+                        staged[depth, start : start + chunk] = gathered_ref[p, k, depth]
                 for start in (0, tile_rows):
-                    copy(staged.at[depth, pl.ds(start, tile_rows)], depth, start, 0)
+                    copy(staged.at[depth, pl.ds(start, tile_rows)], depth, start)
         for each in copies:
             each.wait()
 
@@ -402,11 +409,8 @@
 
     other_source = lax.ppermute(source_field, "tile", swap)
     other_receiver = lax.ppermute(receiver_field, "tile", swap)
-    slow = gather(slowness, "freq")
+    slow = all_slowness(slowness, width)
     terms = first_terms(layouts[0], source_field, receiver_field, other_source, other_receiver)
-    if slow.shape[-1] != LANES:
-        slow = jnp.moveaxis(slow, 0, 2).reshape(STEPS, tile_rows, width // LANES, LANES)
-        slow = jnp.moveaxis(slow, 2, 0)
     other_slow = lax.ppermute(slow, "tile", swap)
 
     chunk = 2 * tile_rows // freqs
@@ -417,7 +421,7 @@
         fields = rest[0] if rest else None
         every.append(maps)
     parts = jnp.stack([maps.reshape(freqs // 2, 2, chunk, width) for maps in every], 2)
-    return tuple(assemble(gather_rows(reduce_rows(parts, "freq"), "freq"), tile_rows, width))
+    return tuple(assemble(sum_rows(parts, "freq"), tile_rows, width))
 
 
 def solution(mesh):

time: 83.5 us -> 77.4 us (0.927)
  waiting for transfers between devices: 34.6 us -> 15.6 us
  blocking collectives: 13.2 us -> 28.7 us
  local copies, waits for them, and re-layouts: 1.67 us -> 0.27 us
  starting transfers between devices: 12.4 us -> 11.4 us
    all_to_all x2 -> x1, waiting for transfers between devices: 22.2 us -> 4.71 us  [gather_rows(): lax.all_to_all(flat, axis, 0, 0, axis_index_groups=groups)]
    all_to_all x1 -> x2, blocking collectives: 13.2 us -> 28.7 us  [the longest x1 14.7 us: sum_rows(): parts = lax.all_to_all(flat, axis, 0, 0, axis_index_groups=groups)]
    all_to_all x2 -> x1, starting transfers between devices: 10.9 us -> 3.73 us  [gather_rows(): lax.all_to_all(flat, axis, 0, 0, axis_index_groups=groups)]
    ppermute x2, starting transfers between devices: 0.94 us -> 7.17 us  [the longest x1 4.1 us: gather_rows(): others = lax.ppermute(rows, axis, between)]
    ppermute x2, waiting for transfers between devices: 12.4 us -> 10.9 us  [the longest x1 8.26 us: sum_rows(): summed = summed + lax.ppermute(summed, axis, between)]
    broadcast_in_dim x2 -> x5, local copies, waits for them, and re-layouts: 1.66 us -> 0.26 us  [the longest x4 0.18 us: gather_rows(): pairs = jnp.where(own, rows, others)]
    another operation x1, other arithmetic: 0.97 us -> 0.07 us  [per_device(): jnp.stack([maps.reshape(freqs // 2, 2, chunk, width) for maps in every], 2)]
  transfers between devices with their start and end apart: 7 -> 6, of which waited for: 4 -> 3; matrix products, arithmetic and copies ran while one was open for 0% -> 0% of each run, Pallas kernels for 6% -> 6%
where the time goes in v2:
time: 77.4 us; the launch traced here: 77.2 us
  blocking collectives  28.7 us (37%)
  Pallas kernels  18.7 us (24%)
  waiting for transfers between devices  15.6 us (20%)
  starting transfers between devices  11.4 us (15%)
  between operations  1.53 us (2%)
  other arithmetic  0.99 us (1%)
    all_to_all x1, blocking collectives, sum_rows(): parts = lax.all_to_all(flat, axis, 0, 0, axis_index_groups=groups)  14.7 us
    all_to_all x1, blocking collectives, sum_rows(): lax.all_to_all(spread, axis, 0, 0, axis_index_groups=groups)  14 us
    pallas_call x2, Pallas kernels, later_depth(): pl.pallas_call(body, out_shape=out_shape, in_specs=[SMEM] + [VMEM] * (len...  10.6 us
    ppermute x1, waiting for transfers between devices, sum_rows(): summed = summed + lax.ppermute(summed, axis, between)  8.26 us
    all_to_all x1, waiting for transfers between devices, gather_rows(): lax.all_to_all(flat, axis, 0, 0, axis_index_groups=groups)  4.71 us
    pallas_call x1, Pallas kernels, first_terms(): pl.pallas_call(body, out_shape=[jax.ShapeDtypeStruct(layout.state(n), jnp...  4.65 us
    ppermute x1, starting transfers between devices, gather_rows(): others = lax.ppermute(rows, axis, between)  4.1 us
    all_to_all x1, starting transfers between devices, gather_rows(): lax.all_to_all(flat, axis, 0, 0, axis_index_groups=groups)  3.73 us
  transfers between devices with their start and end apart: 6, of which 3 were waited for; matrix products, arithmetic and copies ran while one was open for 0% of the time, Pallas kernels for 6%

profile of v2, /device:TPU:0, one launch (start us, length us, event | category | flops | bytes accessed | tf_op | source)
XLA Modules:
  0.0 77.2 jit_solution(16266889886241011004)
XLA Ops:
  0.6 4.1 %collective-permute-start = (f32[3,32,128]{2,1,0:T(8,128)}, f32[3,32,128]{2,1,0:T(8,128)S(1)}, u32[]{:S(2)}, u32[]{:S(2)}) collective-permute-start(f32[3,32,128]{2,1,0:T(8,128)} %param.6), channel_id=1, source_target_pairs={{0,8},{2,10},{4,12},{6,14},{8,0},{10,2},{12,4},{14,6},{1,9},{3,11}... | collective-permute-start | bytes 147464 | tf_op jit(solution)/shard_map/ppermute | solution.py:350
  4.7 0.1 broadcast_in_dim.34
  4.8 0.1 broadcast_in_dim.35
  4.9 0.0 copy-start.2
  4.9 2.6 %collective-permute-done = f32[3,32,128]{2,1,0:T(8,128)S(1)} collective-permute-done((f32[3,32,128]{2,1,0:T(8,128)}, f32[3,32,128]{2,1,0:T(8,128)S(1)}, u32[]{:S(2)}, u32[]{:S(2)}) %collective-permute-start) | collective-permute-done | bytes 49184 | tf_op jit(solution)/shard_map/ppermute | solution.py:350
  7.6 0.0 copy-done.2
  7.6 0.8 %broadcast_select_fusion = f32[4,192,128]{2,1,0:T(8,128)} fusion(f32[192,128]{1,0:T(8,128)S(1)} %bitcast.23, f32[192,128]{1,0:T(8,128)S(1)} %bitcast.24, pred[192]{0:T(512)(128)(4,1)S(1)} %broadcast_in_dim.35), kind=kLoop, calls=%fused_computation.1 | loop fusion | flops 98304 | bytes 590016 | tf_op jit(solution)/shard_map/jit(_where)/select_n | solution.py:352
  8.4 0.0 copy-start
  8.4 0.0 copy-start.1
  8.4 3.7 %all-to-all-start = ((f32[4,192,128]{2,1,0:T(8,128)}), f32[4,192,128]{2,1,0:T(8,128)S(1)}, u32[]{:S(2)}, u32[]{:S(2)}) async-start(f32[4,192,128]{2,1,0:T(8,128)} %broadcast_select_fusion), calls=%async_computation | async-start | bytes 786432 | tf_op jit(solution)/shard_map/all_to_all | solution.py:354
  12.2 0.0 copy-done
  12.2 0.0 collective-permute-start.2
  12.2 0.0 copy-done.1
  12.2 0.5 collective-permute-start.3
  13.3 4.7 %all-to-all-done = f32[4,192,128]{2,1,0:T(8,128)S(1)} async-done(((f32[4,192,128]{2,1,0:T(8,128)}), f32[4,192,128]{2,1,0:T(8,128)S(1)}, u32[]{:S(2)}, u32[]{:S(2)}) %all-to-all-start) | async-done | bytes 393248 | tf_op jit(solution)/shard_map/all_to_all | solution.py:354
  18.0 0.0 collective-permute-start.1
  18.0 0.0 collective-permute-done.2.refs_2_
  18.0 0.0 collective-permute-done.3.refs_3_
  18.0 4.7 %first_terms.1 = (f32[4,8,8,1024]{3,2,1,0:T(8,128)S(1)}, f32[4,8,8,1024]{3,2,1,0:T(8,128)S(1)}, f32[4,8,8,1024]{3,2,1,0:T(8,128)S(1)}, f32[4,7,8,1024]{3,2,1,0:T...) custom-call(f32[2,1,32,1024]{3,2,1,0:T(8,128)S(1)} %copy-done, ...), custom_call_target="tpu_custom_call" | custom-call | flops 8000000000 | bytes 1048576 | tf_op jit(solution)/shard_map/first_terms/pallas_call | solution.py:251
  22.7 0.0 collective-permute-done.1.other_ref.refs_1_
  22.7 2.4 %first_depth.1 = (f32[64,1024]{1,0:T(8,128)S(1)}, f32[4,7,8,1024]{3,2,1,0:T(8,128)S(1)}) custom-call(f32[1]{0:T(128)S(6)} %copy.9.omega_ref, f32[4,2,3,32,128]{4,3,2,1,0:T(8,128)S(1)} %bitcast.16, f32[4,2,3,32,128]{4,3,2,1,0:T(8,128)S(1)} %collective-permute-done.1.other_ref.refs_1_, f32[4,8,8,1024]{3,2,1,0:T(8,128)S(1)} %get-tuple-element.16.refs_0_, ...), custom_call_target="tpu_custom_call" | custom-call | flops 3000000000 | bytes 1048576 | tf_op jit(solution)/shard_map/first_depth/pallas_call | solution.py:276
  25.2 6.1 %later_depth.2 = (f32[64,1024]{1,0:T(8,128)S(1)}, f32[4,6,8,1024]{3,2,1,0:T(8,128)S(1)}) custom-call(f32[1]{0:T(128)S(6)} %copy.9.omega_ref, f32[4,2,3,32,128]{4,3,2,1,0:T(8,128)S(1)} %bitcast.17, f32[4,2,3,32,128]{4,3,2,1,0:T(8,128)S(1)} %collective-permute-done.1.other_ref.refs_1_, f32[4,7,8,1024]{3,2,1,0:T(8,128)S(1)} %get-tuple-element.27.refs_2_), custom_call_target="tpu_custom_call" | custom-call | flops 6000000000 | bytes 1048576 | tf_op jit(solution)/shard_map/later_depth/pallas_call | solution.py:305
  31.2 4.5 %later_depth.3 = f32[64,1024]{1,0:T(8,128)S(1)} custom-call(f32[1]{0:T(128)S(6)} %copy.9.omega_ref, f32[4,2,3,32,128]{4,3,2,1,0:T(8,128)S(1)} %bitcast.18, f32[4,6,8,1024]{3,2,1,0:T(8,128)S(1)} %get-tuple-element.29.refs_1_), custom_call_target="tpu_custom_call" | custom-call | flops 6000000000 | bytes 1048576 | tf_op jit(solution)/shard_map/later_depth/pallas_call | solution.py:305
  35.7 0.1 pad_maximum_fusion
  35.8 14.7 %all_to_all.15 = f32[4,48,1024]{2,1,0:T(8,128)S(1)} all-to-all(f32[4,48,1024]{2,1,0:T(8,128)S(1)} %bitcast.22), channel_id=1, replica_groups={{0,2,4,6},{8,10,12,14},{1,3,5,7},{9,11,13,15},{16,18,20,22},{24,26,28,3..., dimensions={0} | all-to-all | bytes 1572864 | tf_op jit(solution)/shard_map/all_to_all | solution.py:341
  50.5 3.1 %collective-permute-start.4 = (f32[48,1024]{1,0:T(8,128)S(1)}, f32[48,1024]{1,0:T(8,128)S(1)}, u32[]{:S(2)}, u32[]{:S(2)}) collective-permute-start(f32[48,1024]{1,0:T(8,128)S(1)} %reduce_sum.9), channel_id=1, source_target_pairs={{0,8},{2,10},{4,12},{6,14},{8,0},{10,2},{12,4},{14,6},{1,9},{3,11}... | collective-permute-start | bytes 589832 | tf_op jit(solution)/shard_map/ppermute | solution.py:343
  53.6 8.3 %collective-permute-done.4 = f32[48,1024]{1,0:T(8,128)S(1)} collective-permute-done((f32[48,1024]{1,0:T(8,128)S(1)}, f32[48,1024]{1,0:T(8,128)S(1)}, u32[]{:S(2)}, u32[]{:S(2)}) %collective-permute-start.4) | collective-permute-done | bytes 196640 | tf_op jit(solution)/shard_map/ppermute | solution.py:343
  61.9 0.1 broadcast_in_dim.43
  62.0 14.0 %all_to_all.16 = f32[4,48,1024]{2,1,0:T(8,128)S(1)} all-to-all(f32[4,48,1024]{2,1,0:T(8,128)S(1)} %broadcast_in_dim.43), channel_id=1, replica_groups={{0,2,4,6},{8,10,12,14},{1,3,5,7},{9,11,13,15},{16,18,20,22},{24,26,28,3..., dimensions={0} | all-to-all | bytes 1572864 | tf_op jit(solution)/shard_map/all_to_all | solution.py:345
  75.9 1.1 %assemble.1 = (f32[3,32,1024]{2,1,0:T(8,128)}, f32[3,32,1024]{2,1,0:T(8,128)}) custom-call(f32[4,2,3,8,1024]{4,3,2,1,0:T(8,128)S(1)} %bitcast.14), custom_call_target="tpu_custom_call" | custom-call | flops 100000000 | bytes 1048576 | tf_op jit(solution)/shard_map/assemble/pallas_call | solution.py:386
  (5 shorter events, 0.1 us)
Async XLA Ops:
  0.6 6.9 %collective-permute-start = (f32[3,32,128]{2,1,0:T(8,128)}, f32[3,32,128]{2,1,0:T(8,128)S(1)}, u32[]{:S(2)}, u32[]{:S(2)}) collective-permute-start(f32[3,32,128]{2,1,0:T(8,128)} %param.6), channel_id=1, source_target_pairs={{0,8},{2,10},{4,12},{6,14},{8,0},{10,2},{12,4},{14,6},{1,9},{3,11}... | collective-permute-start | bytes 147464 | tf_op jit(solution)/shard_map/ppermute | solution.py:350
  4.9 2.6 %copy-start.2 = (f32[3,32,128]{2,1,0:T(8,128)S(1)}, f32[3,32,128]{2,1,0:T(8,128)}, u32[]{:S(2)}) copy-start(f32[3,32,128]{2,1,0:T(8,128)} %param.6) | copy-start | bytes 147460
  8.4 3.7 %copy-start = (f32[2,1,32,1024]{3,2,1,0:T(8,128)S(1)}, f32[2,1,32,1024]{3,2,1,0:T(8,128)}, u32[]{:S(2)}) copy-start(f32[2,1,32,1024]{3,2,1,0:T(8,128)} %refs_0_.1) | copy-start | bytes 786436
  8.4 3.7 %copy-start.1 = (f32[2,1,32,1024]{3,2,1,0:T(8,128)S(1)}, f32[2,1,32,1024]{3,2,1,0:T(8,128)}, u32[]{:S(2)}) copy-start(f32[2,1,32,1024]{3,2,1,0:T(8,128)} %refs_1_.1) | copy-start | bytes 786436
  8.4 9.6 %all-to-all-start = ((f32[4,192,128]{2,1,0:T(8,128)}), f32[4,192,128]{2,1,0:T(8,128)S(1)}, u32[]{:S(2)}, u32[]{:S(2)}) async-start(f32[4,192,128]{2,1,0:T(8,128)} %broadcast_select_fusion), calls=%async_computation | async-start | bytes 786432 | tf_op jit(solution)/shard_map/all_to_all | solution.py:354
  12.2 5.9 %collective-permute-start.2 = (f32[2,1,32,1024]{3,2,1,0:T(8,128)S(1)}, f32[2,1,32,1024]{3,2,1,0:T(8,128)S(1)}, u32[]{:S(2)}, u32[]{:S(2)}) collective-permute-start(f32[2,1,32,1024]{3,2,1,0:T(8,128)S(1)} %copy-done), channel_id=1, source_target_pairs={{0,1},{1,0},{2,3},{3,2},{4,5},{5,4},{6,7},{7,6},{8,9},{9,8},{10,11... | collective-permute-start | bytes 786440 | tf_op jit(solution)/shard_map/ppermute | solution.py:410
  12.2 5.9 %collective-permute-start.3 = (f32[2,1,32,1024]{3,2,1,0:T(8,128)S(1)}, f32[2,1,32,1024]{3,2,1,0:T(8,128)S(1)}, u32[]{:S(2)}, u32[]{:S(2)}) collective-permute-start(f32[2,1,32,1024]{3,2,1,0:T(8,128)S(1)} %copy-done.1), channel_id=1, source_target_pairs={{0,1},{1,0},{2,3},{3,2},{4,5},{5,4},{6,7},{7,6},{8,9},{9,8},{10,11... | collective-permute-start | bytes 786440 | tf_op jit(solution)/shard_map/ppermute | solution.py:411
  18.0 4.7 %collective-permute-start.1 = (f32[4,2,3,32,128]{4,3,2,1,0:T(8,128)S(1)}, f32[4,2,3,32,128]{4,3,2,1,0:T(8,128)S(1)}, u32[]{:S(2)}, u32[]{:S(2)}) collective-permute-start(f32[4,2,3,32,128]{4,3,2,1,0:T(8,128)S(1)} %bitcast.15), channel_id=1, source_target_pairs={{0,1},{1,0},{2,3},{3,2},{4,5},{5,4},{6,7},{7,6},{8,9},{9,8},{10,11... | collective-permute-start | bytes 1179656 | tf_op jit(solution)/shard_map/ppermute | solution.py:414
  50.5 11.3 %collective-permute-start.4 = (f32[48,1024]{1,0:T(8,128)S(1)}, f32[48,1024]{1,0:T(8,128)S(1)}, u32[]{:S(2)}, u32[]{:S(2)}) collective-permute-start(f32[48,1024]{1,0:T(8,128)S(1)} %reduce_sum.9), channel_id=1, source_target_pairs={{0,8},{2,10},{4,12},{6,14},{8,0},{10,2},{12,4},{14,6},{1,9},{3,11}... | collective-permute-start | bytes 589832 | tf_op jit(solution)/shard_map/ppermute | solution.py:343

commit v3 on v2

--- a/solution.py
+++ b/solution.py
@@ -151,36 +151,35 @@
     columns = range(layout.columns)
 
     def one_pass(n, c):
-            source, count, have = terms[n - 1], layout.blocks(n), layout.blocks(n - 1)
-            here = [source[c, 0, :, cols(j)] for j in columns]
-            here_up = [pltpu.roll(x, ROWS - 1, 0) for x in here]
-            before = here
-            for b in range(count):
-                if b + 1 < have:
-                    below = [source[c, b + 1, :, cols(j)] for j in columns]
-                    below_up = [pltpu.roll(x, ROWS - 1, 0) for x in below]
-                else:
-                    below = below_up = [zero] * layout.columns
-                pairs = [p + jnp.where(row_last, q, r) for p, q, r in zip(here, below_up, here_up)]
-                pairs_down = [pltpu.roll(u, 1, 0) for u in pairs]
-                x = [u + jnp.where(row_first, q, r) for u, q, r in zip(pairs, before, pairs_down)]
-                before = pairs_down
-                x_left = [pltpu.roll(v, LANES - 1, 1) for v in x] + [zero]
-                x_right = [pltpu.roll(v, 1, 1) for v in x] + [zero]
-                wide = [
-                    (x[j] + x[j])
-                    + (
-                        jnp.where(lane_last, x_left[j + 1], x_left[j])
-                        + jnp.where(lane_first, x_right[j - 1], x_right[j])
-                    )
-                    for j in columns
-                ]
-                for j in columns:
-                    value = wide[j] - 8.0 * here[j]
-                    if n % 2 == 0 and ROOTS[n // 2 - 1] != 0.0:
-                        value = value - (64.0 * ROOTS[n // 2 - 1]) * terms[n - 2][c, b, :, cols(j)]
-                    terms[n][c, b, :, cols(j)] = value
-                here, here_up = below, below_up
+        source, count, have = terms[n - 1], layout.blocks(n), layout.blocks(n - 1)
+
+        def tile(b, j):
+            return source[c, b, :, cols(j)] if b < have else zero
+
+        up = [pltpu.roll(tile(0, j), ROWS - 1, 0) for j in columns]
+        before = [None] * layout.columns
+        for b in range(count):
+            x, left, right = {}, {-1: zero}, {layout.columns: zero}
+
+            def finish(j, b=b, x=x, left=left, right=right):
+                low = jnp.where(lane_first, left[j - 1], left[j])
+                high = jnp.where(lane_last, right[j + 1], right[j])
+                value = (x[j] + x[j]) + (low + high) - 8.0 * tile(b, j)
+                if n % 2 == 0 and ROOTS[n // 2 - 1] != 0.0:
+                    value = value - (64.0 * ROOTS[n // 2 - 1]) * terms[n - 2][c, b, :, cols(j)]
+                terms[n][c, b, :, cols(j)] = value
+
+            for j in columns:
+                p = tile(b, j)
+                below = pltpu.roll(tile(b + 1, j), ROWS - 1, 0)
+                pair = p + jnp.where(row_last, below, up[j])
+                down = pltpu.roll(pair, 1, 0)
+                x[j] = pair + jnp.where(row_first, p if b == 0 else before[j], down)
+                up[j], before[j] = below, down
+                left[j], right[j] = pltpu.roll(x[j], 1, 1), pltpu.roll(x[j], LANES - 1, 1)
+                if j > 0:
+                    finish(j - 1)
+            finish(layout.columns - 1)
 
     for n in range(1, TERMS):
         for c in range(4):

time: 77.4 us -> 77.3 us (level)
  no operation moved by 1% of the time
where the time goes in v3:
time: 77.3 us; the launch traced here: 77 us
  blocking collectives  28.7 us (37%)
  Pallas kernels  18.6 us (24%)
  waiting for transfers between devices  15.6 us (20%)
  starting transfers between devices  11.4 us (15%)
  between operations  1.53 us (2%)
  other arithmetic  0.99 us (1%)
    all_to_all x1, blocking collectives, sum_rows(): parts = lax.all_to_all(flat, axis, 0, 0, axis_index_groups=groups)  14.7 us
    all_to_all x1, blocking collectives, sum_rows(): lax.all_to_all(spread, axis, 0, 0, axis_index_groups=groups)  14 us
    pallas_call x2, Pallas kernels, later_depth(): pl.pallas_call(body, out_shape=out_shape, in_specs=[SMEM] + [VMEM] * (len...  10.5 us
    ppermute x1, waiting for transfers between devices, sum_rows(): summed = summed + lax.ppermute(summed, axis, between)  8.26 us
    all_to_all x1, waiting for transfers between devices, gather_rows(): lax.all_to_all(flat, axis, 0, 0, axis_index_groups=groups)  4.71 us
    pallas_call x1, Pallas kernels, first_terms(): pl.pallas_call(body, out_shape=[jax.ShapeDtypeStruct(layout.state(n), jnp...  4.56 us
    ppermute x1, starting transfers between devices, gather_rows(): others = lax.ppermute(rows, axis, between)  4.1 us
    all_to_all x1, starting transfers between devices, gather_rows(): lax.all_to_all(flat, axis, 0, 0, axis_index_groups=groups)  3.73 us
  transfers between devices with their start and end apart: 6, of which 3 were waited for; matrix products, arithmetic and copies ran while one was open for 0% of the time, Pallas kernels for 6%

profile of v3, /device:TPU:0, one launch (start us, length us, event | category | flops | bytes accessed | tf_op | source)
XLA Modules:
  0.0 77.0 jit_solution(6406685092324450681)
XLA Ops:
  0.6 4.1 %collective-permute-start = (f32[3,32,128]{2,1,0:T(8,128)}, f32[3,32,128]{2,1,0:T(8,128)S(1)}, u32[]{:S(2)}, u32[]{:S(2)}) collective-permute-start(f32[3,32,128]{2,1,0:T(8,128)} %param.6), channel_id=1, source_target_pairs={{0,8},{2,10},{4,12},{6,14},{8,0},{10,2},{12,4},{14,6},{1,9},{3,11}... | collective-permute-start | bytes 147464 | tf_op jit(solution)/shard_map/ppermute | solution.py:349
  4.7 0.1 broadcast_in_dim.34
  4.8 0.1 broadcast_in_dim.35
  4.9 0.0 copy-start.2
  4.9 2.6 %collective-permute-done = f32[3,32,128]{2,1,0:T(8,128)S(1)} collective-permute-done((f32[3,32,128]{2,1,0:T(8,128)}, f32[3,32,128]{2,1,0:T(8,128)S(1)}, u32[]{:S(2)}, u32[]{:S(2)}) %collective-permute-start) | collective-permute-done | bytes 49184 | tf_op jit(solution)/shard_map/ppermute | solution.py:349
  7.6 0.0 copy-done.2
  7.6 0.8 %broadcast_select_fusion = f32[4,192,128]{2,1,0:T(8,128)} fusion(f32[192,128]{1,0:T(8,128)S(1)} %bitcast.23, f32[192,128]{1,0:T(8,128)S(1)} %bitcast.24, pred[192]{0:T(512)(128)(4,1)S(1)} %broadcast_in_dim.35), kind=kLoop, calls=%fused_computation.1 | loop fusion | flops 98304 | bytes 590016 | tf_op jit(solution)/shard_map/jit(_where)/select_n | solution.py:351
  8.4 0.0 copy-start
  8.4 0.0 copy-start.1
  8.4 3.7 %all-to-all-start = ((f32[4,192,128]{2,1,0:T(8,128)}), f32[4,192,128]{2,1,0:T(8,128)S(1)}, u32[]{:S(2)}, u32[]{:S(2)}) async-start(f32[4,192,128]{2,1,0:T(8,128)} %broadcast_select_fusion), calls=%async_computation | async-start | bytes 786432 | tf_op jit(solution)/shard_map/all_to_all | solution.py:353
  12.2 0.0 copy-done
  12.2 0.0 collective-permute-start.2
  12.2 0.0 copy-done.1
  12.2 0.5 collective-permute-start.3
  13.3 4.7 %all-to-all-done = f32[4,192,128]{2,1,0:T(8,128)S(1)} async-done(((f32[4,192,128]{2,1,0:T(8,128)}), f32[4,192,128]{2,1,0:T(8,128)S(1)}, u32[]{:S(2)}, u32[]{:S(2)}) %all-to-all-start) | async-done | bytes 393248 | tf_op jit(solution)/shard_map/all_to_all | solution.py:353
  18.0 0.0 collective-permute-start.1
  18.0 0.0 collective-permute-done.2.refs_2_
  18.0 0.0 collective-permute-done.3.refs_3_
  18.0 4.6 %first_terms.1 = (f32[4,8,8,1024]{3,2,1,0:T(8,128)S(1)}, f32[4,8,8,1024]{3,2,1,0:T(8,128)S(1)}, f32[4,8,8,1024]{3,2,1,0:T(8,128)S(1)}, f32[4,7,8,1024]{3,2,1,0:T...) custom-call(f32[2,1,32,1024]{3,2,1,0:T(8,128)S(1)} %copy-done, ...), custom_call_target="tpu_custom_call" | custom-call | flops 8000000000 | bytes 1048576 | tf_op jit(solution)/shard_map/first_terms/pallas_call | solution.py:250
  22.6 0.0 collective-permute-done.1.other_ref.refs_1_
  22.6 2.4 %first_depth.1 = (f32[64,1024]{1,0:T(8,128)S(1)}, f32[4,7,8,1024]{3,2,1,0:T(8,128)S(1)}) custom-call(f32[1]{0:T(128)S(6)} %copy.9.omega_ref, f32[4,2,3,32,128]{4,3,2,1,0:T(8,128)S(1)} %bitcast.16, f32[4,2,3,32,128]{4,3,2,1,0:T(8,128)S(1)} %collective-permute-done.1.other_ref.refs_1_, f32[4,8,8,1024]{3,2,1,0:T(8,128)S(1)} %get-tuple-element.16.refs_0_, ...), custom_call_target="tpu_custom_call" | custom-call | flops 3000000000 | bytes 1048576 | tf_op jit(solution)/shard_map/first_depth/pallas_call | solution.py:275
  25.1 6.1 %later_depth.2 = (f32[64,1024]{1,0:T(8,128)S(1)}, f32[4,6,8,1024]{3,2,1,0:T(8,128)S(1)}) custom-call(f32[1]{0:T(128)S(6)} %copy.9.omega_ref, f32[4,2,3,32,128]{4,3,2,1,0:T(8,128)S(1)} %bitcast.17, f32[4,2,3,32,128]{4,3,2,1,0:T(8,128)S(1)} %collective-permute-done.1.other_ref.refs_1_, f32[4,7,8,1024]{3,2,1,0:T(8,128)S(1)} %get-tuple-element.27.refs_2_), custom_call_target="tpu_custom_call" | custom-call | flops 6000000000 | bytes 1048576 | tf_op jit(solution)/shard_map/later_depth/pallas_call | solution.py:304
  31.1 4.5 %later_depth.3 = f32[64,1024]{1,0:T(8,128)S(1)} custom-call(f32[1]{0:T(128)S(6)} %copy.9.omega_ref, f32[4,2,3,32,128]{4,3,2,1,0:T(8,128)S(1)} %bitcast.18, f32[4,6,8,1024]{3,2,1,0:T(8,128)S(1)} %get-tuple-element.29.refs_1_), custom_call_target="tpu_custom_call" | custom-call | flops 6000000000 | bytes 1048576 | tf_op jit(solution)/shard_map/later_depth/pallas_call | solution.py:304
  35.6 0.1 pad_maximum_fusion
  35.7 14.7 %all_to_all.15 = f32[4,48,1024]{2,1,0:T(8,128)S(1)} all-to-all(f32[4,48,1024]{2,1,0:T(8,128)S(1)} %bitcast.22), channel_id=1, replica_groups={{0,2,4,6},{8,10,12,14},{1,3,5,7},{9,11,13,15},{16,18,20,22},{24,26,28,3..., dimensions={0} | all-to-all | bytes 1572864 | tf_op jit(solution)/shard_map/all_to_all | solution.py:340
  50.4 3.1 %collective-permute-start.4 = (f32[48,1024]{1,0:T(8,128)S(1)}, f32[48,1024]{1,0:T(8,128)S(1)}, u32[]{:S(2)}, u32[]{:S(2)}) collective-permute-start(f32[48,1024]{1,0:T(8,128)S(1)} %reduce_sum.9), channel_id=1, source_target_pairs={{0,8},{2,10},{4,12},{6,14},{8,0},{10,2},{12,4},{14,6},{1,9},{3,11}... | collective-permute-start | bytes 589832 | tf_op jit(solution)/shard_map/ppermute | solution.py:342
  53.5 8.3 %collective-permute-done.4 = f32[48,1024]{1,0:T(8,128)S(1)} collective-permute-done((f32[48,1024]{1,0:T(8,128)S(1)}, f32[48,1024]{1,0:T(8,128)S(1)}, u32[]{:S(2)}, u32[]{:S(2)}) %collective-permute-start.4) | collective-permute-done | bytes 196640 | tf_op jit(solution)/shard_map/ppermute | solution.py:342
  61.8 0.1 broadcast_in_dim.43
  61.8 14.0 %all_to_all.16 = f32[4,48,1024]{2,1,0:T(8,128)S(1)} all-to-all(f32[4,48,1024]{2,1,0:T(8,128)S(1)} %broadcast_in_dim.43), channel_id=1, replica_groups={{0,2,4,6},{8,10,12,14},{1,3,5,7},{9,11,13,15},{16,18,20,22},{24,26,28,3..., dimensions={0} | all-to-all | bytes 1572864 | tf_op jit(solution)/shard_map/all_to_all | solution.py:344
  75.8 1.1 %assemble.1 = (f32[3,32,1024]{2,1,0:T(8,128)}, f32[3,32,1024]{2,1,0:T(8,128)}) custom-call(f32[4,2,3,8,1024]{4,3,2,1,0:T(8,128)S(1)} %bitcast.14), custom_call_target="tpu_custom_call" | custom-call | flops 100000000 | bytes 1048576 | tf_op jit(solution)/shard_map/assemble/pallas_call | solution.py:385
  (5 shorter events, 0.1 us)
Async XLA Ops:
  0.6 6.9 %collective-permute-start = (f32[3,32,128]{2,1,0:T(8,128)}, f32[3,32,128]{2,1,0:T(8,128)S(1)}, u32[]{:S(2)}, u32[]{:S(2)}) collective-permute-start(f32[3,32,128]{2,1,0:T(8,128)} %param.6), channel_id=1, source_target_pairs={{0,8},{2,10},{4,12},{6,14},{8,0},{10,2},{12,4},{14,6},{1,9},{3,11}... | collective-permute-start | bytes 147464 | tf_op jit(solution)/shard_map/ppermute | solution.py:349
  4.9 2.6 %copy-start.2 = (f32[3,32,128]{2,1,0:T(8,128)S(1)}, f32[3,32,128]{2,1,0:T(8,128)}, u32[]{:S(2)}) copy-start(f32[3,32,128]{2,1,0:T(8,128)} %param.6) | copy-start | bytes 147460
  8.4 3.7 %copy-start = (f32[2,1,32,1024]{3,2,1,0:T(8,128)S(1)}, f32[2,1,32,1024]{3,2,1,0:T(8,128)}, u32[]{:S(2)}) copy-start(f32[2,1,32,1024]{3,2,1,0:T(8,128)} %refs_0_.1) | copy-start | bytes 786436
  8.4 3.7 %copy-start.1 = (f32[2,1,32,1024]{3,2,1,0:T(8,128)S(1)}, f32[2,1,32,1024]{3,2,1,0:T(8,128)}, u32[]{:S(2)}) copy-start(f32[2,1,32,1024]{3,2,1,0:T(8,128)} %refs_1_.1) | copy-start | bytes 786436
  8.4 9.6 %all-to-all-start = ((f32[4,192,128]{2,1,0:T(8,128)}), f32[4,192,128]{2,1,0:T(8,128)S(1)}, u32[]{:S(2)}, u32[]{:S(2)}) async-start(f32[4,192,128]{2,1,0:T(8,128)} %broadcast_select_fusion), calls=%async_computation | async-start | bytes 786432 | tf_op jit(solution)/shard_map/all_to_all | solution.py:353
  12.2 5.9 %collective-permute-start.2 = (f32[2,1,32,1024]{3,2,1,0:T(8,128)S(1)}, f32[2,1,32,1024]{3,2,1,0:T(8,128)S(1)}, u32[]{:S(2)}, u32[]{:S(2)}) collective-permute-start(f32[2,1,32,1024]{3,2,1,0:T(8,128)S(1)} %copy-done), channel_id=1, source_target_pairs={{0,1},{1,0},{2,3},{3,2},{4,5},{5,4},{6,7},{7,6},{8,9},{9,8},{10,11... | collective-permute-start | bytes 786440 | tf_op jit(solution)/shard_map/ppermute | solution.py:409
  12.2 5.9 %collective-permute-start.3 = (f32[2,1,32,1024]{3,2,1,0:T(8,128)S(1)}, f32[2,1,32,1024]{3,2,1,0:T(8,128)S(1)}, u32[]{:S(2)}, u32[]{:S(2)}) collective-permute-start(f32[2,1,32,1024]{3,2,1,0:T(8,128)S(1)} %copy-done.1), channel_id=1, source_target_pairs={{0,1},{1,0},{2,3},{3,2},{4,5},{5,4},{6,7},{7,6},{8,9},{9,8},{10,11... | collective-permute-start | bytes 786440 | tf_op jit(solution)/shard_map/ppermute | solution.py:410
  18.0 4.6 %collective-permute-start.1 = (f32[4,2,3,32,128]{4,3,2,1,0:T(8,128)S(1)}, f32[4,2,3,32,128]{4,3,2,1,0:T(8,128)S(1)}, u32[]{:S(2)}, u32[]{:S(2)}) collective-permute-start(f32[4,2,3,32,128]{4,3,2,1,0:T(8,128)S(1)} %bitcast.15), channel_id=1, source_target_pairs={{0,1},{1,0},{2,3},{3,2},{4,5},{5,4},{6,7},{7,6},{8,9},{9,8},{10,11... | collective-permute-start | bytes 1179656 | tf_op jit(solution)/shard_map/ppermute | solution.py:413
  50.4 11.3 %collective-permute-start.4 = (f32[48,1024]{1,0:T(8,128)S(1)}, f32[48,1024]{1,0:T(8,128)S(1)}, u32[]{:S(2)}, u32[]{:S(2)}) collective-permute-start(f32[48,1024]{1,0:T(8,128)S(1)} %reduce_sum.9), channel_id=1, source_target_pairs={{0,8},{2,10},{4,12},{6,14},{8,0},{10,2},{12,4},{14,6},{1,9},{3,11}... | collective-permute-start | bytes 589832 | tf_op jit(solution)/shard_map/ppermute | solution.py:342
